TPU v7x, 32 devices: a whole 2x2x4 slice. The times are simulated.
32 devices in a mesh: dom: 2 (over y), row: 4 (over z), feat: 4 (over x, core).
Axes of the slice: x: 2, y: 2, z: 4, core: 2. Of those that a mesh axis runs over, the one named last changes fastest.
Arguments:
- feats: bfloat16 [65536, 768], P(('dom', 'row'), 'feat'), parts along dimension 0, may hold values from -6 to 6
- req_rows: int32 [8, 1536], P(('dom', 'row')), parts along dimension 0, may hold values from 0 to 8191
- req_slots: int32 [8, 1536], P(('dom', 'row')), parts along dimension 0, may hold values from 0 to 3199
- block_count: int32 [8, 4], P(('dom', 'row')), parts along dimension 0, may hold values from 1 to 3, as said below
- rel_weight: bfloat16 [6, 768, 1024], P(None, 'feat'), may hold values from -0.21875 to 0.21875
- bias: float32 [1024], replicated, may hold values from -3 to 3
- gain: float32 [1024], replicated, may hold values from 0.5 to 1.5
- offset: float32 [1024], replicated, may hold values from -3 to 3
Outputs:
- hidden: bfloat16 [5120, 1024], P(('dom', 'row', 'feat')), parts along dimension 0
There are 2 independent parts, one for each index of `dom`. A program takes and returns all parts, laid end to end along the dimension named above; an argument that names none is the same for every part. Nothing has to cross between parts.
Inputs may be any that keep to these rules, and one draw needn't show every extreme that they name: `req_rows`: a row index on the owner of its block. `req_slots`: t * 5 + r for a target t of the asking device and a relation r. Only the first block_count * 128 of the 384 slots a device keeps for an owner are live; in every draw some owner receives 3 blocks from every device.
All inputs are finite; a program needn't handle non-finite values.
Results may differ from a plain program's by a relative error of at most 0.0019.
Values may be sent and summed in bfloat16 or wider, within the bound.
A program may use at most 128 MiB of HBM per device.

v0:
```python
import jax
import jax.numpy as jnp
from jax import lax
from jax.sharding import PartitionSpec as P

REL = 5
BLK = 128
TGT_DEV = 640


epsilon = 1e-05


def body(feats, req_rows, req_slots, block_count, rel_weight, bias, gain, offset):
    owners = lax.axis_size("row")
    columns = feats.shape[1]
    hidden_width = rel_weight.shape[2]
    per_owner = req_rows.shape[1] // owners
    outgoing = req_rows.reshape(owners, per_owner)
    found_rows = jnp.take(
        feats, lax.all_to_all(outgoing, "row", split_axis=0, concat_axis=0, tiled=True), axis=0
    )
    fetched = lax.all_to_all(found_rows, "row", split_axis=0, concat_axis=0, tiled=True)
    slot_pos = lax.broadcasted_iota(jnp.int32, (owners, per_owner), 1)
    live_slots = (slot_pos < block_count.reshape(owners, 1) * BLK).reshape(-1).astype(jnp.float32)
    segments = req_slots.reshape(-1)
    counts = jax.ops.segment_sum(live_slots, segments, num_segments=TGT_DEV * REL)
    weights_slot = live_slots / jnp.maximum(counts, 1.0)[segments]
    summed = jax.ops.segment_sum(
        fetched.reshape(-1, columns).astype(jnp.float32) * weights_slot[:, None],
        segments,
        num_segments=TGT_DEV * REL,
    )
    mean_rows = summed.astype(jnp.bfloat16).reshape(TGT_DEV, REL * columns)
    operand = jnp.concatenate([mean_rows, feats[:TGT_DEV]], axis=1)
    flat_weight = rel_weight.reshape((REL + 1) * columns, hidden_width)
    partial_terms = jnp.dot(operand, flat_weight, preferred_element_type=jnp.float32)
    projected = lax.psum_scatter(partial_terms, "feat", scatter_dimension=1, tiled=True)
    piece_cols = projected.shape[1]
    first_col = lax.axis_index("feat") * piece_cols
    bias_cols = lax.dynamic_slice_in_dim(bias, first_col, piece_cols, 0)
    gain_cols = lax.dynamic_slice_in_dim(gain, first_col, piece_cols, 0)
    offset_cols = lax.dynamic_slice_in_dim(offset, first_col, piece_cols, 0)
    activated = jnp.maximum(projected + bias_cols, 0.0)
    row_mean = lax.psum(jnp.sum(activated, axis=1), "feat") / hidden_width
    deviation = activated - row_mean[:, None]
    row_spread = lax.psum(jnp.sum(deviation * deviation, axis=1), "feat") / hidden_width
    normed = (
        deviation * lax.rsqrt(row_spread + epsilon)[:, None] * gain_cols + offset_cols
    ).astype(jnp.bfloat16)
    return lax.all_to_all(normed, "feat", split_axis=0, concat_axis=1, tiled=True)


def solution(mesh):
    return jax.shard_map(
        body,
        mesh=mesh,
        in_specs=(
            P(("dom", "row"), "feat"),
            P(("dom", "row"), None),
            P(("dom", "row"), None),
            P(("dom", "row"), None),
            P(None, "feat", None),
            P(),
            P(),
            P(),
        ),
        out_specs=P(("dom", "row", "feat"), None),
        check_vma=False,
    )
```

profile of v0, /device:TPU:0, one launch (start us, length us, event | category | flops | bytes accessed | tf_op | source)
XLA Modules:
  0.0 144.0 jit_solution(11151635200367157774)
XLA Ops:
  6.5 0.0 copy-start
  6.5 6.4 %all-to-all-start = ((s32[4,1,384]{2,1,0:T(1,128)}), s32[4,1,384]{2,1,0:T(1,128)S(1)}, u32[]{:S(2)}, u32[]{:S(2)}) async-start(s32[4,1,384]{2,1,0:T(1,128)} %bitcast.26), calls=%async_computation | async-start | bytes 12288 | tf_op jit(solution)/shard_map/all_to_all | solution.py:21
  13.0 5.9 %copy.24 = bf16[8192,192]{1,0:T(8,128)(2,1)} copy(bf16[8192,192]{0,1:T(8,128)(2,1)} %param.8) | data formatting | bytes 6291456 | tf_op args[0]
  18.9 0.0 all-to-all-done
  19.0 6.4 %gather_fusion = bf16[1536,192]{1,0:T(8,128)(2,1)S(1)} fusion(bf16[8192,192]{1,0:T(8,128)(2,1)} %copy.24, s32[2048]{0:T(1024)S(1)} %pad_clamp_fusion.1), kind=kCustom, calls=%fused_computation | custom fusion | bytes 1185792 | tf_op jit(solution)/shard_map/jit(_take)/gather | solution.py:20
  25.3 0.0 copy-start.3
  25.4 0.0 copy-start.2
  25.4 1.1 copy.25
  26.5 2.0 %broadcast_select_fusion = bf16[4,384,192]{1,2,0:T(8,128)(2,1)} fusion(bf16[4,384,192]{1,2,0:T(8,128)(2,1)} %copy.25, pred[4,384]{1,0:T(4,128)(4,1)S(1)} %compare_and_fusion), kind=kLoop, calls=%fused_computation.15 | loop fusion | flops 294912 | bytes 1181184 | tf_op jit(solution)/shard_map/jit(_take)/select_n | solution.py:20
  28.4 5.1 %all-to-all-start.1 = ((bf16[4,384,192]{1,2,0:T(8,128)(2,1)}), bf16[4,384,192]{1,2,0:T(8,128)(2,1)S(1)}, u32[]{:S(2)}, u32[]{:S(2)}) async-start(bf16[4,384,192]{1,2,0:T(8,128)(2,1)} %broadcast_select_fusion), calls=%async_computation.1 | async-start | bytes 1179648 | tf_op jit(solution)/shard_map/all_to_all | solution.py:23
  33.5 0.0 reduce-scatter.2.cloned.1.call-start
  33.5 0.0 copy-done.3
  33.5 0.1 fusion.11
  33.6 0.0 copy-done.2
  33.7 8.6 %scatter_custom_fusion = f32[3200]{0:T(1024)S(1)} fusion(s32[1536]{0:T(1024)S(1)} %reduce, f32[1536]{0:T(1024)S(1)} %reshape.137, f32[]{:T(128)} %constant.13.clone.1), kind=kCustom, calls=%fused_computation.23 | custom fusion | flops 1536 | bytes 12804 | tf_op jit(solution)/shard_map/scatter-add | solution.py:27
  42.3 8.4 %gather_fusion.1 = f32[1536]{0:T(1024)S(1)} fusion(f32[3200]{0:T(1024)S(1)} %broadcast_maximum_fusion, s32[2048]{0:T(1024)S(1)} %pad_clamp_fusion), kind=kCustom, calls=%fused_computation.1 | custom fusion | bytes 18432 | tf_op jit(solution)/shard_map/gather | solution.py:28
  50.7 0.0 all-to-all-done.1
  50.7 0.1 convert_bitcast_fusion
  50.8 0.1 copy.31
  51.0 0.1 broadcast_multiply_fusion
  51.1 1.7 %copy.27 = f32[1536,192]{1,0:T(8,128)} copy(f32[1536,192]{0,1:T(8,128)S(1)} %broadcast_multiply_fusion) | data formatting | bytes 2359296 | tf_op jit(solution)/shard_map/mul | solution.py:30
  52.8 11.1 %scatter_custom_fusion.1 = f32[3200,192]{1,0:T(8,128)} fusion(s32[1536]{0:T(1024)S(1)} %reduce, f32[1536,192]{1,0:T(8,128)} %copy.27, f32[]{:T(128)} %constant.13.clone.1), kind=kCustom, calls=%fused_computation.4 | custom fusion | flops 294912 | bytes 2458112 | tf_op jit(solution)/shard_map/scatter-add | solution.py:29
  63.9 3.4 %convert_element_type.26 = bf16[3200,192]{1,0:T(8,128)(2,1)} convert(f32[3200,192]{1,0:T(8,128)} %scatter_custom_fusion.1) | non-fusion elementwise | flops 614400 | bytes 3686400 | tf_op jit(solution)/shard_map/convert_element_type | solution.py:34
  67.3 0.0 slice-start
  67.3 4.1 %reshape.113 = bf16[640,960]{1,0:T(8,128)(2,1)} reshape(bf16[3200,192]{1,0:T(8,128)(2,1)} %convert_element_type.26) | data formatting | bytes 2457600 | tf_op jit(solution)/shard_map/reshape | solution.py:34
  71.4 0.0 copy-done
  71.4 0.0 slice-done
  71.4 4.7 %fusion.2 = f32[640,1024]{1,0:T(8,128)} fusion(bf16[1152,1024]{1,0:T(8,128)(2,1)S(1)} %bitcast.21, bf16[640,192]{1,0:T(8,128)(2,1)S(1)} %slice-done, bf16[640,960]{1,0:T(8,128)(2,1)} %reshape.113), kind=kOutput, calls=%fused_computation.6 | convolution fusion | flops 1512898560 | bytes 6455296 | tf_op jit(solution)/shard_map/dot_general | solution.py:37
  76.1 0.0 reduce-scatter.2.cloned.1.call-update
  76.1 0.8 dynamic_slice.11
  76.9 0.8 dynamic_slice.10
  77.7 0.8 dynamic_slice.9
  78.4 34.0 %reduce-scatter.2.cloned.1.call-done = f32[640,256]{1,0:T(8,128)} async-done(((f32[640,1024]{1,0:T(8,128)}), f32[640,256]{1,0:T(8,128)}) %reduce-scatter.2.cloned.1.call-update) | async-done | bytes 655376 | tf_op jit(solution)/shard_map/reduce_scatter | solution.py:38
  112.4 0.0 copy-start.1
  112.4 1.3 fusion.6
  113.8 5.8 %psum.14 = f32[640]{0:T(1024)S(1)} all-reduce(f32[640]{0:T(1024)S(1)} %fusion.6), channel_id=1, replica_groups=mesh['dom'=2,'row'=4,'feat'=4] {'feat'}, use_global_device_ids=true, to_apply=%region_4.5 | all-reduce | flops 640 | bytes 5120 | tf_op jit(solution)/shard_map/psum | solution.py:45
  119.5 1.4 multiply_reduce_fusion
  120.9 5.7 %psum.15 = f32[640]{0:T(1024)S(1)} all-reduce(f32[640]{0:T(1024)S(1)} %multiply_reduce_fusion), channel_id=1, replica_groups=mesh['dom'=2,'row'=4,'feat'=4] {'feat'}, use_global_device_ids=true, to_apply=%region_6.7 | all-reduce | flops 640 | bytes 5120 | tf_op jit(solution)/shard_map/psum | solution.py:47
  126.6 0.0 copy-done.1
  126.6 0.2 add_convert_fusion
  126.8 9.6 %all_to_all.39 = bf16[4,160,256]{2,1,0:T(8,128)(2,1)S(1)} all-to-all(bf16[4,160,256]{2,1,0:T(8,128)(2,1)S(1)} %bitcast.24), channel_id=1, replica_groups=mesh['dom'=2,'row'=4,'feat'=4] {'feat'}, dimensions={0} | all-to-all | bytes 655360 | tf_op jit(solution)/shard_map/all_to_all | solution.py:51
  136.4 0.8 copy.32
  (13 shorter events, 0.2 us)
Async XLA Ops:
  6.5 64.9 %copy-start = (bf16[6,192,1024]{2,1,0:T(8,128)(2,1)S(1)}, bf16[6,192,1024]{2,1,0:T(8,128)(2,1)}, u32[]{:S(2)}) copy-start(bf16[6,192,1024]{2,1,0:T(8,128)(2,1)} %param.12) | copy-start | bytes 7077892
  6.5 12.4 %all-to-all-start = ((s32[4,1,384]{2,1,0:T(1,128)}), s32[4,1,384]{2,1,0:T(1,128)S(1)}, u32[]{:S(2)}, u32[]{:S(2)}) async-start(s32[4,1,384]{2,1,0:T(1,128)} %bitcast.26), calls=%async_computation | async-start | bytes 12288 | tf_op jit(solution)/shard_map/all_to_all | solution.py:21
  25.3 8.2 %copy-start.3 = (s32[1,4]{1,0:T(1,128)S(1)}, s32[1,4]{1,0:T(1,128)}, u32[]{:S(2)}) copy-start(s32[1,4]{1,0:T(1,128)} %param.11) | copy-start | bytes 52
  25.4 8.3 %copy-start.2 = (s32[1,1536]{1,0:T(1,128)S(1)}, s32[1,1536]{1,0:T(1,128)}, u32[]{:S(2)}) copy-start(s32[1,1536]{1,0:T(1,128)} %param.10) | copy-start | bytes 18436
  28.4 22.3 %all-to-all-start.1 = ((bf16[4,384,192]{1,2,0:T(8,128)(2,1)}), bf16[4,384,192]{1,2,0:T(8,128)(2,1)S(1)}, u32[]{:S(2)}, u32[]{:S(2)}) async-start(bf16[4,384,192]{1,2,0:T(8,128)(2,1)} %broadcast_select_fusion), calls=%async_computation.1 | async-start | bytes 1179648 | tf_op jit(solution)/shard_map/all_to_all | solution.py:23
  33.5 78.9 %reduce-scatter.2.cloned.1.call-start = ((), (), s32[]{:S(2)}) async-start(), calls=%async_computation.4 | async-start | bytes 3276800 | tf_op jit(solution)/shard_map/reduce_scatter | solution.py:38
  67.3 4.1 %slice-start = ((bf16[8192,192]{1,0:T(8,128)(2,1)}), bf16[640,192]{1,0:T(8,128)(2,1)S(1)}, s32[]{:S(2)}) async-start(bf16[8192,192]{1,0:T(8,128)(2,1)} %copy.24), calls=%async_computation.5 | async-start | bytes 655360 | tf_op jit(solution)/shard_map/slice | solution.py:35
  112.4 14.1 %copy-start.1 = (f32[640,256]{1,0:T(8,128)S(1)}, f32[640,256]{1,0:T(8,128)}, u32[]{:S(2)}) copy-start(f32[640,256]{1,0:T(8,128)} %reduce-scatter.2.cloned.1.call-done) | copy-start | bytes 1966084
Sparse Core Ops, SparseCore 0:
  76.2 36.1 reduce-scatter.1
where the time goes:
time: 145 us; the launch traced here: 144 us
  waiting for transfers between devices  34 us (23%)
  local copies, waits for them, and re-layouts  30.9 us (21%)
  other arithmetic  28.3 us (20%)
  blocking collectives  21 us (14%)
  between operations  13.5 us (9%)
  starting transfers between devices  11.5 us (8%)
  matrix products  4.68 us (3%)
    reduce_scatter x1, waiting for transfers between devices, body(): lax.psum_scatter(partial_terms, 'feat', scatter_dimension=1, tiled=True)  34 us
    scatter-add x1, other arithmetic, body(): jax.ops.segment_sum(fetched.reshape(-1, columns).astype(jnp.float32) * we...  11.1 us
    all_to_all x1, blocking collectives, body(): lax.all_to_all(normed, 'feat', split_axis=0, concat_axis=1, tiled=True)  9.57 us
    scatter-add x1, other arithmetic, body(): jax.ops.segment_sum(live_slots, segments, num_segments=TGT_DEV * REL)  8.59 us
    gather x1, local copies, waits for them, and re-layouts, body(): weights_slot = live_slots / jnp.maximum(counts, 1.0)[segments]  8.39 us
    gather x2, local copies, waits for them, and re-layouts, body(): jnp.take(feats, lax.all_to_all(outgoing, 'row', split_axis=0, concat_axis...  7.48 us
    all_to_all x1, starting transfers between devices, body(): lax.all_to_all(outgoing, 'row', split_axis=0, concat_axis=0, tiled=True)  6.45 us
    unnamed x9, local copies, waits for them, and re-layouts  5.93 us
  transfers between devices with their start and end apart: 3, of which 1 were waited for; matrix products, arithmetic and copies ran while one was open for 18% of the time, Pallas kernels for 0%

commit v1 on v0

v1 whole, which is shorter than its diff:
```python
import functools

import jax
import jax.numpy as jnp
from jax import lax
from jax.experimental import pallas as pl
from jax.experimental.pallas import tpu as pltpu
from jax.sharding import PartitionSpec as P

REL = 5
BLK = 128
MESH = pl.DeviceIdType.MESH
F32 = jnp.float32
BF16 = jnp.bfloat16

epsilon = 1e-05

FEAT_CHUNKS = 8
CAST_ROWS = 256
GATHER_UNROLL = 16
COL_PIECES = 4


def kernel(
    owners, bc_ref, rows_ref, slots_ref, feats_ref, weight_ref, bias_ref, gain_ref, offset_ref,
    out_ref,
    asked, feats_v, feats_f, weight_v, found, sent, got, block, agg, own_term, operand,
    part, half_in, half_out, last_in,
    asked_send, asked_recv, feats_sem, weight_sem, own_sem, row_send, row_recv,
    pair_send, pair_recv, far_send, far_recv,
):
    me = lax.axis_index("row")
    place = lax.axis_index("feat")
    high, low = place // 2, place % 2
    pair = {"feat": high * 2 + 1 - low}
    far = {"feat": (1 - high) * 2 + low}
    nodes, columns = feats_v.shape
    asks = slots_ref.shape[1] // owners
    half = asks // 2
    steps = owners - 1
    rows_out, width = out_ref.shape
    piece = width // COL_PIECES

    def shift(step):
        return 1 + lax.rem(owners // 2 - 1 + step, steps)

    def dest_of(step):
        return lax.rem(me + shift(step), owners)

    def owner_of(step):
        return lax.rem(me - shift(step) + owners, owners)

    def my_rows(owner):
        return rows_ref.at[:, pl.ds(pl.multiple_of(owner * asks, BLK), asks)]

    chunk_rows = nodes // FEAT_CHUNKS

    def feats_copy(c):
        span = pl.ds(pl.multiple_of(c * chunk_rows, chunk_rows), chunk_rows)
        return pltpu.make_async_copy(feats_ref.at[span, :], feats_v.at[span, :], feats_sem.at[c])

    for c in range(FEAT_CHUNKS):
        feats_copy(c).start()
    own_copy = pltpu.make_async_copy(my_rows(me), asked.at[steps], own_sem)
    own_copy.start()
    weight_copy = pltpu.make_async_copy(weight_ref, weight_v, weight_sem)
    weight_copy.start()

    barrier = pltpu.get_barrier_semaphore()

    @pl.loop(0, steps)
    def _(step):
        pl.semaphore_signal(barrier, inc=1, device_id={"row": dest_of(step)}, device_id_type=MESH)

    pl.semaphore_signal(barrier, inc=1, device_id=pair, device_id_type=MESH)
    pl.semaphore_signal(barrier, inc=1, device_id=far, device_id_type=MESH)
    pl.semaphore_wait(barrier, steps + 2)

    def ask(step):
        owner = owner_of(step)
        return pltpu.make_async_remote_copy(
            src_ref=my_rows(owner), dst_ref=asked.at[step],
            send_sem=asked_send.at[step], recv_sem=asked_recv.at[step],
            device_id={"row": owner}, device_id_type=MESH,
        )

    def answer(step):
        return pltpu.make_async_remote_copy(
            src_ref=sent.at[step], dst_ref=got.at[step],
            send_sem=row_send.at[step], recv_sem=row_recv.at[step],
            device_id={"row": dest_of(step)}, device_id_type=MESH,
        )

    @pl.loop(0, steps)
    def _(step):
        ask(step).start()

    @pl.loop(0, FEAT_CHUNKS)
    def _(c):
        feats_copy(c).wait()

        @pl.loop(0, chunk_rows // CAST_ROWS)
        def _(i):
            span = pl.ds(pl.multiple_of(c * chunk_rows + i * CAST_ROWS, CAST_ROWS), CAST_ROWS)
            feats_f[span, :] = feats_v[span, :].astype(F32)

    def gather(step, put):
        @pl.loop(0, asks // GATHER_UNROLL)
        def _(g):
            base = pl.multiple_of(g * GATHER_UNROLL, GATHER_UNROLL)
            for u in range(GATHER_UNROLL):
                node = asked[step, 0, base + u]
                found[pl.ds(base + u, 1), :] = feats_f[pl.ds(node, 1), :]

        put(slice(0, asks), found[:, :BLK].astype(BF16))
        tail = columns - BLK
        first = found[pl.ds(0, half), BLK:columns]
        second = found[pl.ds(half, half), BLK:columns]
        put(slice(asks, asks + half), jnp.concatenate([first, second], axis=1).astype(BF16))

    @pl.loop(0, steps)
    def _(step):
        ask(step).wait_recv()

        def put(span, value):
            sent[step, span, :] = value

        gather(step, put)
        answer(step).start()

    own_copy.wait()

    def put_own(span, value):
        got[steps, span, :] = value

    gather(steps, put_own)

    weight_copy.wait()

    @pl.loop(0, 4)
    def _(c):
        span = pl.ds(pl.multiple_of(c * rows_out, rows_out), rows_out)
        own_term[c] = jnp.dot(feats_v[span, :], weight_v[REL], preferred_element_type=F32)

    lane = lax.broadcasted_iota(jnp.int32, (asks, BLK), 1)

    def unpack(step):
        block[:, :BLK] = got[step, :asks, :]
        tails = got[step, asks:, :].astype(F32)
        both = jnp.concatenate([tails, pltpu.roll(tails, BLK // 2, 1)], axis=0)
        block[:, BLK:] = jnp.where(lane == columns - BLK, 1.0, both).astype(BF16)

    pos = lax.broadcasted_iota(jnp.int32, (1, asks), 1)

    def keys_of(owner):
        keys = slots_ref[:, pl.ds(pl.multiple_of(owner * asks, BLK), asks)]
        return jnp.where(pos < bc_ref[0, owner] * BLK, keys, -1)

    target = lax.broadcasted_iota(jnp.int32, (rows_out, asks), 0) * REL

    def sums(keys, chunk, rel):
        hits = target == keys - (chunk * rows_out * REL + rel)
        pick = jnp.where(hits, 1.0, 0.0).astype(BF16)
        return jnp.dot(pick, block[...], preferred_element_type=F32)

    unpack(steps)
    own_keys = keys_of(me)

    @pl.loop(0, 4)
    def _(chunk):
        for rel in range(REL):
            agg[chunk, rel] = sums(own_keys, chunk, rel)

    @pl.loop(0, steps - 1)
    def _(step):
        answer(step).wait_recv()
        unpack(step)
        keys = keys_of(owner_of(step))

        @pl.loop(0, 4)
        def _(chunk):
            for rel in range(REL):
                agg[chunk, rel] += sums(keys, chunk, rel)

    answer(steps - 1).wait_recv()
    unpack(steps - 1)
    last_keys = keys_of(owner_of(steps - 1))

    def operands(chunk):
        for rel in range(REL):
            total = agg[chunk, rel] + sums(last_keys, chunk, rel)
            count = total[:, columns:columns + 1]
            mean = total[:, :columns] * (1.0 / jnp.maximum(count, 1.0))
            operand[rel] = mean.astype(BF16)

    def project(chunk, q):
        cols = slice(q * piece, (q + 1) * piece)
        value = own_term[chunk, :, cols]
        for rel in range(REL):
            value += jnp.dot(operand[rel], weight_v[rel, :, cols], preferred_element_type=F32)
        return value

    def to_pair(i, q):
        return pltpu.make_async_remote_copy(
            src_ref=part.at[i, q], dst_ref=half_in.at[i, q],
            send_sem=pair_send.at[i, q], recv_sem=pair_recv.at[i, q],
            device_id=pair, device_id_type=MESH,
        )

    def to_far(q):
        return pltpu.make_async_remote_copy(
            src_ref=half_out.at[q], dst_ref=last_in.at[q],
            send_sem=far_send.at[q], recv_sem=far_recv.at[q],
            device_id=far, device_id_type=MESH,
        )

    chunk = (1 - high) * 2 + 1 - low
    operands(chunk)
    for q in range(COL_PIECES):
        part[0, q] = project(chunk, q)
        to_pair(0, q).start()

    chunk = (1 - high) * 2 + low
    operands(chunk)
    for q in range(COL_PIECES):
        value = project(chunk, q)
        to_pair(0, q).wait_recv()
        half_out[q] = value + half_in[0, q]
        to_far(q).start()

    chunk = high * 2 + 1 - low
    operands(chunk)
    for q in range(COL_PIECES):
        part[1, q] = project(chunk, q)
        to_pair(1, q).start()

    chunk = high * 2 + low
    operands(chunk)
    for q in range(COL_PIECES):
        cols = slice(q * piece, (q + 1) * piece)
        value = project(chunk, q)
        to_pair(1, q).wait_recv()
        own_term[chunk, :, cols] = value + half_in[1, q] + bias_ref[:, cols]

    total = jnp.zeros((rows_out, 1), F32)
    for q in range(COL_PIECES):
        cols = slice(q * piece, (q + 1) * piece)
        to_far(q).wait_recv()
        act = jnp.maximum(own_term[chunk, :, cols] + last_in[q], 0.0)
        last_in[q] = act
        total += jnp.sum(act, axis=1, keepdims=True)
    mu = total / width
    spread = jnp.zeros((rows_out, 1), F32)
    for q in range(COL_PIECES):
        dev = last_in[q] - mu
        spread += jnp.sum(dev * dev, axis=1, keepdims=True)
    scale = lax.rsqrt(spread / width + epsilon)
    for q in range(COL_PIECES):
        cols = slice(q * piece, (q + 1) * piece)
        dev = last_in[q] - mu
        out_ref[:, cols] = (dev * scale * gain_ref[:, cols] + offset_ref[:, cols]).astype(BF16)

    @pl.loop(0, steps)
    def _(step):
        ask(step).wait_send()
        answer(step).wait_send()

    for q in range(COL_PIECES):
        to_pair(0, q).wait_send()
        to_pair(1, q).wait_send()
        to_far(q).wait_send()


def body(feats, req_rows, req_slots, block_count, rel_weight, bias, gain, offset):
    owners = lax.axis_size("row")
    ranks = lax.axis_size("feat")
    nodes, columns = feats.shape
    rels, _, width = rel_weight.shape
    asks = req_rows.shape[1] // owners
    steps = owners - 1
    rows_out = 640 // ranks
    piece = width // COL_PIECES
    packed = asks + asks // 2
    dma = pltpu.SemaphoreType.DMA
    vmem = pl.BlockSpec(memory_space=pltpu.VMEM)
    hbm = pl.BlockSpec(memory_space=pl.ANY)
    return pl.pallas_call(
        functools.partial(kernel, owners),
        out_shape=jax.ShapeDtypeStruct((rows_out, width), BF16),
        in_specs=[pl.BlockSpec(memory_space=pltpu.SMEM), hbm, vmem, hbm, hbm, vmem, vmem, vmem],
        out_specs=vmem,
        scratch_shapes=[
            pltpu.SMEM((owners, 1, asks), jnp.int32),
            pltpu.VMEM((nodes, columns), BF16),
            pltpu.VMEM((nodes, columns), F32),
            pltpu.VMEM((rels, columns, width), BF16),
            pltpu.VMEM((asks, columns), F32),
            pltpu.VMEM((steps, packed, BLK), BF16),
            pltpu.VMEM((owners, packed, BLK), BF16),
            pltpu.VMEM((asks, 2 * BLK), BF16),
            pltpu.VMEM((ranks, REL, rows_out, 2 * BLK), F32),
            pltpu.VMEM((ranks, rows_out, width), F32),
            pltpu.VMEM((REL, rows_out, columns), BF16),
            pltpu.VMEM((2, COL_PIECES, rows_out, piece), F32),
            pltpu.VMEM((2, COL_PIECES, rows_out, piece), F32),
            pltpu.VMEM((COL_PIECES, rows_out, piece), F32),
            pltpu.VMEM((COL_PIECES, rows_out, piece), F32),
            dma((steps,)), dma((steps,)), dma((FEAT_CHUNKS,)), dma, dma,
            dma((steps,)), dma((steps,)),
            dma((2, COL_PIECES)), dma((2, COL_PIECES)),
            dma((COL_PIECES,)), dma((COL_PIECES,)),
        ],
        compiler_params=pltpu.CompilerParams(
            collective_id=0, has_side_effects=True, vmem_limit_bytes=48 * 1024 * 1024
        ),
        name="rgcn",
    )(
        block_count, req_rows, req_slots, feats, rel_weight,
        bias.reshape(1, -1), gain.reshape(1, -1), offset.reshape(1, -1),
    )


def solution(mesh):
    return jax.shard_map(
        body,
        mesh=mesh,
        in_specs=(
            P(("dom", "row"), "feat"),
            P(("dom", "row"), None),
            P(("dom", "row"), None),
            P(("dom", "row"), None),
            P(None, "feat", None),
            P(),
            P(),
            P(),
        ),
        out_specs=P(("dom", "row", "feat"), None),
        check_vma=False,
    )
```

time: 145 us -> 51.6 us (0.36)
  Pallas kernels: 0 us -> 44.5 us
  waiting for transfers between devices: 34 us -> 0 us
  other arithmetic: 28.3 us -> 0 us
  local copies, waits for them, and re-layouts: 30.9 us -> 6.85 us
  blocking collectives: 21 us -> 0 us
  between operations: 13.5 us -> 0.07 us
  starting transfers between devices: 11.5 us -> 0 us
  matrix products: 4.68 us -> 0 us
    pallas_call x0 -> x1, Pallas kernels: none -> 44.5 us  [body(): pl.pallas_call(functools.partial(kernel, owners), out_shape=jax.ShapeDtyp...]
    reduce_scatter x1 -> x0, waiting for transfers between devices: 34 us -> none  [body(): lax.psum_scatter(partial_terms, 'feat', scatter_dimension=1, tiled=True)]
    scatter-add x2 -> x0, other arithmetic: 19.7 us -> none  [the longest x1 11.1 us: body(): jax.ops.segment_sum(fetched.reshape(-1, columns).astype(jnp.float32) * we...]
    gather x3 -> x0, local copies, waits for them, and re-layouts: 15.9 us -> none  [the longest x1 8.39 us: body(): weights_slot = live_slots / jnp.maximum(counts, 1.0)[segments]]
    all_to_all x2 -> x0, starting transfers between devices: 11.5 us -> none  [the longest x1 6.45 us: body(): lax.all_to_all(outgoing, 'row', split_axis=0, concat_axis=0, tiled=True)]
    psum x2 -> x0, blocking collectives: 11.4 us -> none  [the longest x1 5.77 us: body(): row_mean = lax.psum(jnp.sum(activated, axis=1), 'feat') / hidden_width]
    all_to_all x1 -> x0, blocking collectives: 9.57 us -> none  [body(): lax.all_to_all(normed, 'feat', split_axis=0, concat_axis=1, tiled=True)]
    dot_general x1 -> x0, matrix products: 4.68 us -> none  [body(): jnp.dot(operand, flat_weight, preferred_element_type=jnp.float32)]
  transfers between devices with their start and end apart: 3 -> 0, of which waited for: 1 -> 0; matrix products, arithmetic and copies ran while one was open for 18% -> 0% of each run, Pallas kernels for 0% -> 0%
where the time goes in v1:
time: 51.6 us; the launch traced here: 51.4 us
  Pallas kernels  44.5 us (86%)
  local copies, waits for them, and re-layouts  6.85 us (13%)
    pallas_call x1, Pallas kernels, body(): pl.pallas_call(functools.partial(kernel, owners), out_shape=jax.ShapeDtyp...  44.5 us
    unnamed x16, local copies, waits for them, and re-layouts  6.85 us

profile of v1, /device:TPU:0, one launch (start us, length us, event | category | flops | bytes accessed | tf_op | source)
XLA Modules:
  0.0 51.4 jit_solution(4159134313657699643)
XLA Ops:
  0.0 0.0 copy-start
  0.0 0.0 copy-start.1
  0.0 0.0 copy-start.2
  0.0 0.0 copy-start.3
  0.0 0.0 copy-start.4
  0.0 0.0 copy-start.5
  0.0 0.0 copy-start.6
  0.0 6.1 %copy.9.feats_ref = bf16[8192,192]{1,0:T(8,128)(2,1)} copy(bf16[8192,192]{0,1:T(8,128)(2,1)} %param.8) | data formatting | bytes 6291456 | tf_op args[0]
  6.1 0.0 copy-done
  6.1 0.0 copy-done.1
  6.1 0.0 copy-done.2
  6.1 0.0 copy-done.3
  6.1 0.0 copy-done.4
  6.2 0.0 copy-done.5
  6.2 0.0 copy-done.6
  6.2 44.5 %rgcn.1 = bf16[160,1024]{1,0:T(8,128)(2,1)S(1)} custom-call(s32[1,4]{1,0:T(1,128)S(1)} %copy-done.6, s32[1,1536]{1,0:T(1,128)S(1)} %copy-done.1, s32[1,1536]{1,0:T(1,128)S(1)} %copy-done.2, bf16[8192,192]{1,0:T(8,128)(2,1)} %copy.9.feats_ref, bf16[6,192,1024]{2,1,0:T(8,128)(2,1)S(1)} %copy-done, f32[1,1024]{1,0:T(1,128)S(1)} %bitcast.3, ...), custom_call_target="tpu_custom_call" | custom-call | tf_op jit(solution)/shard_map/rgcn/pallas_call | solution.py:287
  50.7 0.7 %copy.11 = bf16[160,1024]{1,0:T(8,128)(2,1)} copy(bf16[160,1024]{1,0:T(8,128)(2,1)S(1)} %rgcn.1) | data formatting | bytes 655360
Async XLA Ops:
  0.0 6.1 %copy-start = (bf16[6,192,1024]{2,1,0:T(8,128)(2,1)S(1)}, bf16[6,192,1024]{2,1,0:T(8,128)(2,1)}, u32[]{:S(2)}) copy-start(bf16[6,192,1024]{2,1,0:T(8,128)(2,1)} %weight_ref.1) | copy-start | bytes 7077892
  0.0 6.1 %copy-start.1 = (s32[1,1536]{1,0:T(1,128)S(1)}, s32[1,1536]{1,0:T(1,128)}, u32[]{:S(2)}) copy-start(s32[1,1536]{1,0:T(1,128)} %rows_ref.1) | copy-start | bytes 18436
  0.0 6.1 %copy-start.2 = (s32[1,1536]{1,0:T(1,128)S(1)}, s32[1,1536]{1,0:T(1,128)}, u32[]{:S(2)}) copy-start(s32[1,1536]{1,0:T(1,128)} %slots_ref.1) | copy-start | bytes 18436
  0.0 6.1 %copy-start.3 = (f32[1024]{0:T(1024)S(1)}, f32[1024]{0:T(1024)}, u32[]{:S(2)}) copy-start(f32[1024]{0:T(1024)} %param.13) | copy-start | bytes 12292
  0.0 6.1 %copy-start.4 = (f32[1024]{0:T(1024)S(1)}, f32[1024]{0:T(1024)}, u32[]{:S(2)}) copy-start(f32[1024]{0:T(1024)} %param.14) | copy-start | bytes 12292
  0.0 6.1 %copy-start.5 = (f32[1024]{0:T(1024)S(1)}, f32[1024]{0:T(1024)}, u32[]{:S(2)}) copy-start(f32[1024]{0:T(1024)} %param.15) | copy-start | bytes 12292
  0.0 6.1 %copy-start.6 = (s32[1,4]{1,0:T(1,128)S(1)}, s32[1,4]{1,0:T(1,128)}, u32[]{:S(2)}) copy-start(s32[1,4]{1,0:T(1,128)} %bc_ref.1) | copy-start | bytes 52

commit v2 on v1

--- a/solution.py
+++ b/solution.py
@@ -34,7 +34,7 @@
     high, low = place // 2, place % 2
     pair = {"feat": high * 2 + 1 - low}
     far = {"feat": (1 - high) * 2 + low}
-    nodes, columns = feats_v.shape
+    nodes, columns = feats_f.shape
     asks = slots_ref.shape[1] // owners
     half = asks // 2
     steps = owners - 1
@@ -57,7 +57,7 @@
 
     def feats_copy(c):
         span = pl.ds(pl.multiple_of(c * chunk_rows, chunk_rows), chunk_rows)
-        return pltpu.make_async_copy(feats_ref.at[span, :], feats_v.at[span, :], feats_sem.at[c])
+        return pltpu.make_async_copy(feats_ref.at[:, span], feats_v.at[:, span], feats_sem.at[c])
 
     for c in range(FEAT_CHUNKS):
         feats_copy(c).start()
@@ -95,14 +95,19 @@
     def _(step):
         ask(step).start()
 
+    unit_row = lax.broadcasted_iota(jnp.int32, (CAST_ROWS, CAST_ROWS), 0)
+    unit_col = lax.broadcasted_iota(jnp.int32, (CAST_ROWS, CAST_ROWS), 1)
+    unit = jnp.where(unit_row == unit_col, 1.0, 0.0).astype(BF16)
+
     @pl.loop(0, FEAT_CHUNKS)
     def _(c):
         feats_copy(c).wait()
 
-        @pl.loop(0, chunk_rows // CAST_ROWS)
-        def _(i):
+        for i in range(chunk_rows // CAST_ROWS):
             span = pl.ds(pl.multiple_of(c * chunk_rows + i * CAST_ROWS, CAST_ROWS), CAST_ROWS)
-            feats_f[span, :] = feats_v[span, :].astype(F32)
+            feats_f[span, :] = lax.dot_general(
+                unit, feats_v[:, span], (((1,), (1,)), ((), ())), preferred_element_type=F32
+            )
 
     def gather(step, put):
         @pl.loop(0, asks // GATHER_UNROLL)
@@ -140,7 +145,7 @@
     @pl.loop(0, 4)
     def _(c):
         span = pl.ds(pl.multiple_of(c * rows_out, rows_out), rows_out)
-        own_term[c] = jnp.dot(feats_v[span, :], weight_v[REL], preferred_element_type=F32)
+        own_term[c] = jnp.dot(feats_f[span, :].astype(BF16), weight_v[REL], preferred_element_type=F32)
 
     lane = lax.broadcasted_iota(jnp.int32, (asks, BLK), 1)
 
@@ -291,7 +296,7 @@
         out_specs=vmem,
         scratch_shapes=[
             pltpu.SMEM((owners, 1, asks), jnp.int32),
-            pltpu.VMEM((nodes, columns), BF16),
+            pltpu.VMEM((columns, nodes), BF16),
             pltpu.VMEM((nodes, columns), F32),
             pltpu.VMEM((rels, columns, width), BF16),
             pltpu.VMEM((asks, columns), F32),
@@ -311,11 +316,11 @@
             dma((COL_PIECES,)), dma((COL_PIECES,)),
         ],
         compiler_params=pltpu.CompilerParams(
-            collective_id=0, has_side_effects=True, vmem_limit_bytes=48 * 1024 * 1024
+            collective_id=0, has_side_effects=True, vmem_limit_bytes=60 * 1024 * 1024
         ),
         name="rgcn",
     )(
-        block_count, req_rows, req_slots, feats, rel_weight,
+        block_count, req_rows, req_slots, feats.T, rel_weight,
         bias.reshape(1, -1), gain.reshape(1, -1), offset.reshape(1, -1),
     )
 

time: 51.6 us -> 47.4 us (0.919)
  local copies, waits for them, and re-layouts: 6.85 us -> 1.72 us
  Pallas kernels: 44.5 us -> 45.5 us
    unnamed x16 -> x1, local copies, waits for them, and re-layouts: 6.85 us -> 1.72 us
    pallas_call x1, Pallas kernels: 44.5 us -> 45.5 us  [body(): pl.pallas_call(functools.partial(kernel, owners), out_shape=jax.ShapeDtyp...]
where the time goes in v2:
time: 47.4 us; the launch traced here: 47.2 us
  Pallas kernels  45.5 us (96%)
  local copies, waits for them, and re-layouts  1.72 us (4%)
    pallas_call x1, Pallas kernels, body(): pl.pallas_call(functools.partial(kernel, owners), out_shape=jax.ShapeDtyp...  45.5 us
    unnamed x1, local copies, waits for them, and re-layouts  1.72 us

profile of v2, /device:TPU:0, one launch (start us, length us, event | category | flops | bytes accessed | tf_op | source)
XLA Modules:
  0.0 47.2 jit_solution(12521410861604731683)
XLA Ops:
  0.0 45.5 %rgcn.1 = bf16[160,1024]{1,0:T(8,128)(2,1)} custom-call(s32[1,4]{1,0:T(1,128)} %bc_ref.1, s32[1,1536]{1,0:T(1,128)} %rows_ref.1, s32[1,1536]{1,0:T(1,128)} %slots_ref.1, bf16[192,8192]{1,0:T(8,128)(2,1)} %bitcast.4, bf16[6,192,1024]{2,1,0:T(8,128)(2,1)} %weight_ref.1, f32[1,1024]{1,0:T(1,128)} %bitcast.5, f32[1,1024]{1,0:T(1,128)} %bitcast.6, f32[1,1024]{1,0:T(1,128)} %bitcast.7), custom_call_target="tpu_custom_call" | custom-call | tf_op jit(solution)/shard_map/rgcn/pallas_call | solution.py:292
  45.5 1.7 %copy.10 = bf16[160,1024]{1,0:T(8,128)(2,1)} copy(bf16[160,1024]{1,0:T(8,128)(2,1)} %rgcn.1) | data formatting | bytes 655360

commit v3 on v2

--- a/solution.py
+++ b/solution.py
@@ -19,15 +19,17 @@
 CAST_ROWS = 256
 GATHER_UNROLL = 16
 COL_PIECES = 4
+LEVELS = 32767.0
+TINY = 1e-30
 
 
 def kernel(
     owners, bc_ref, rows_ref, slots_ref, feats_ref, weight_ref, bias_ref, gain_ref, offset_ref,
     out_ref,
     asked, feats_v, feats_f, weight_v, found, sent, got, block, agg, own_term, operand,
-    part, half_in, half_out, last_in,
+    part, half_in, half_out, half_scale, last_in, last_scale, acted,
     asked_send, asked_recv, feats_sem, weight_sem, own_sem, row_send, row_recv,
-    pair_send, pair_recv, far_send, far_recv,
+    pair_send, pair_recv, far_send, far_recv, scale_send, scale_recv,
 ):
     me = lax.axis_index("row")
     place = lax.axis_index("feat")
@@ -219,6 +221,24 @@
             device_id=far, device_id_type=MESH,
         )
 
+    def scale_to_far(q):
+        return pltpu.make_async_remote_copy(
+            src_ref=half_scale.at[q], dst_ref=last_scale.at[q],
+            send_sem=scale_send.at[q], recv_sem=scale_recv.at[q],
+            device_id=far, device_id_type=MESH,
+        )
+
+    def encode(q, value):
+        top = jnp.maximum(jnp.max(jnp.abs(value), axis=1, keepdims=True), TINY)
+        step = jnp.broadcast_to(top * (1.0 / LEVELS), (rows_out, BLK))
+        half_scale[q] = jnp.transpose(step)[:1, :]
+        half_out[q] = jnp.round(value * (LEVELS / top)).astype(jnp.int32).astype(jnp.int16)
+
+    def decode(q):
+        step = jnp.transpose(jnp.broadcast_to(last_scale[q], (BLK, rows_out)))
+        step = jnp.concatenate([step] * (piece // BLK), axis=1)
+        return last_in[q].astype(jnp.int32).astype(F32) * step
+
     chunk = (1 - high) * 2 + 1 - low
     operands(chunk)
     for q in range(COL_PIECES):
@@ -230,7 +250,8 @@
     for q in range(COL_PIECES):
         value = project(chunk, q)
         to_pair(0, q).wait_recv()
-        half_out[q] = value + half_in[0, q]
+        encode(q, value + half_in[0, q])
+        scale_to_far(q).start()
         to_far(q).start()
 
     chunk = high * 2 + 1 - low
@@ -250,19 +271,20 @@
     total = jnp.zeros((rows_out, 1), F32)
     for q in range(COL_PIECES):
         cols = slice(q * piece, (q + 1) * piece)
+        scale_to_far(q).wait_recv()
         to_far(q).wait_recv()
-        act = jnp.maximum(own_term[chunk, :, cols] + last_in[q], 0.0)
-        last_in[q] = act
+        act = jnp.maximum(own_term[chunk, :, cols] + decode(q), 0.0)
+        acted[q] = act
         total += jnp.sum(act, axis=1, keepdims=True)
     mu = total / width
     spread = jnp.zeros((rows_out, 1), F32)
     for q in range(COL_PIECES):
-        dev = last_in[q] - mu
+        dev = acted[q] - mu
         spread += jnp.sum(dev * dev, axis=1, keepdims=True)
     scale = lax.rsqrt(spread / width + epsilon)
     for q in range(COL_PIECES):
         cols = slice(q * piece, (q + 1) * piece)
-        dev = last_in[q] - mu
+        dev = acted[q] - mu
         out_ref[:, cols] = (dev * scale * gain_ref[:, cols] + offset_ref[:, cols]).astype(BF16)
 
     @pl.loop(0, steps)
@@ -273,6 +295,7 @@
     for q in range(COL_PIECES):
         to_pair(0, q).wait_send()
         to_pair(1, q).wait_send()
+        scale_to_far(q).wait_send()
         to_far(q).wait_send()
 
 
@@ -308,12 +331,15 @@
             pltpu.VMEM((REL, rows_out, columns), BF16),
             pltpu.VMEM((2, COL_PIECES, rows_out, piece), F32),
             pltpu.VMEM((2, COL_PIECES, rows_out, piece), F32),
-            pltpu.VMEM((COL_PIECES, rows_out, piece), F32),
+            pltpu.VMEM((COL_PIECES, rows_out, piece), jnp.int16),
+            pltpu.VMEM((COL_PIECES, 1, rows_out), F32),
+            pltpu.VMEM((COL_PIECES, rows_out, piece), jnp.int16),
+            pltpu.VMEM((COL_PIECES, 1, rows_out), F32),
             pltpu.VMEM((COL_PIECES, rows_out, piece), F32),
             dma((steps,)), dma((steps,)), dma((FEAT_CHUNKS,)), dma, dma,
             dma((steps,)), dma((steps,)),
             dma((2, COL_PIECES)), dma((2, COL_PIECES)),
-            dma((COL_PIECES,)), dma((COL_PIECES,)),
+            dma((COL_PIECES,)), dma((COL_PIECES,)), dma((COL_PIECES,)), dma((COL_PIECES,)),
         ],
         compiler_params=pltpu.CompilerParams(
             collective_id=0, has_side_effects=True, vmem_limit_bytes=60 * 1024 * 1024

time: 47.4 us -> 40.7 us (0.86)
  Pallas kernels: 45.5 us -> 38.8 us
    pallas_call x1, Pallas kernels: 45.5 us -> 38.8 us  [body(): pl.pallas_call(functools.partial(kernel, owners), out_shape=jax.ShapeDtyp...]
where the time goes in v3:
time: 40.7 us; the launch traced here: 40.5 us
  Pallas kernels  38.8 us (95%)
  local copies, waits for them, and re-layouts  1.72 us (4%)
    pallas_call x1, Pallas kernels, body(): pl.pallas_call(functools.partial(kernel, owners), out_shape=jax.ShapeDtyp...  38.8 us
    unnamed x1, local copies, waits for them, and re-layouts  1.72 us

profile of v3, /device:TPU:0, one launch (start us, length us, event | category | flops | bytes accessed | tf_op | source)
XLA Modules:
  0.0 40.5 jit_solution(4360177693426068462)
XLA Ops:
  0.0 38.8 %rgcn.1 = bf16[160,1024]{1,0:T(8,128)(2,1)} custom-call(s32[1,4]{1,0:T(1,128)} %bc_ref.1, s32[1,1536]{1,0:T(1,128)} %rows_ref.1, s32[1,1536]{1,0:T(1,128)} %slots_ref.1, bf16[192,8192]{1,0:T(8,128)(2,1)} %bitcast.4, bf16[6,192,1024]{2,1,0:T(8,128)(2,1)} %weight_ref.1, f32[1,1024]{1,0:T(1,128)} %bitcast.5, f32[1,1024]{1,0:T(1,128)} %bitcast.6, f32[1,1024]{1,0:T(1,128)} %bitcast.7), custom_call_target="tpu_custom_call" | custom-call | tf_op jit(solution)/shard_map/rgcn/pallas_call | solution.py:315
  38.8 1.7 %copy.10 = bf16[160,1024]{1,0:T(8,128)(2,1)} copy(bf16[160,1024]{1,0:T(8,128)(2,1)} %rgcn.1) | data formatting | bytes 655360

commit v4 on v3

--- a/solution.py
+++ b/solution.py
@@ -19,6 +19,7 @@
 CAST_ROWS = 256
 GATHER_UNROLL = 16
 COL_PIECES = 4
+SHARES = 2
 LEVELS = 32767.0
 TINY = 1e-30
 
@@ -38,7 +39,8 @@
     far = {"feat": (1 - high) * 2 + low}
     nodes, columns = feats_f.shape
     asks = slots_ref.shape[1] // owners
-    half = asks // 2
+    share = asks // SHARES
+    half = share // 2
     steps = owners - 1
     rows_out, width = out_ref.shape
     piece = width // COL_PIECES
@@ -86,10 +88,10 @@
             device_id={"row": owner}, device_id_type=MESH,
         )
 
-    def answer(step):
-        return pltpu.make_async_remote_copy(
-            src_ref=sent.at[step], dst_ref=got.at[step],
-            send_sem=row_send.at[step], recv_sem=row_recv.at[step],
+    def answer(step, k):
+        return pltpu.make_async_remote_copy(
+            src_ref=sent.at[step, k], dst_ref=got.at[step, k],
+            send_sem=row_send.at[step, k], recv_sem=row_recv.at[step, k],
             device_id={"row": dest_of(step)}, device_id_type=MESH,
         )
 
@@ -111,36 +113,29 @@
                 unit, feats_v[:, span], (((1,), (1,)), ((), ())), preferred_element_type=F32
             )
 
-    def gather(step, put):
-        @pl.loop(0, asks // GATHER_UNROLL)
+    def gather(step, k, to):
+        @pl.loop(0, share // GATHER_UNROLL)
         def _(g):
             base = pl.multiple_of(g * GATHER_UNROLL, GATHER_UNROLL)
             for u in range(GATHER_UNROLL):
-                node = asked[step, 0, base + u]
+                node = asked[step, 0, k * share + base + u]
                 found[pl.ds(base + u, 1), :] = feats_f[pl.ds(node, 1), :]
 
-        put(slice(0, asks), found[:, :BLK].astype(BF16))
-        tail = columns - BLK
-        first = found[pl.ds(0, half), BLK:columns]
-        second = found[pl.ds(half, half), BLK:columns]
-        put(slice(asks, asks + half), jnp.concatenate([first, second], axis=1).astype(BF16))
+        to[step, k, :share, :] = found[:, :BLK].astype(BF16)
+        first = found[:half, BLK:]
+        second = found[half:, BLK:]
+        to[step, k, share:, :] = jnp.concatenate([first, second], axis=1).astype(BF16)
 
     @pl.loop(0, steps)
     def _(step):
         ask(step).wait_recv()
-
-        def put(span, value):
-            sent[step, span, :] = value
-
-        gather(step, put)
-        answer(step).start()
+        for k in range(SHARES):
+            gather(step, k, sent)
+            answer(step, k).start()
 
     own_copy.wait()
-
-    def put_own(span, value):
-        got[steps, span, :] = value
-
-    gather(steps, put_own)
+    for k in range(SHARES):
+        gather(steps, k, got)
 
     weight_copy.wait()
 
@@ -149,13 +144,15 @@
         span = pl.ds(pl.multiple_of(c * rows_out, rows_out), rows_out)
         own_term[c] = jnp.dot(feats_f[span, :].astype(BF16), weight_v[REL], preferred_element_type=F32)
 
-    lane = lax.broadcasted_iota(jnp.int32, (asks, BLK), 1)
-
-    def unpack(step):
-        block[:, :BLK] = got[step, :asks, :]
-        tails = got[step, asks:, :].astype(F32)
-        both = jnp.concatenate([tails, pltpu.roll(tails, BLK // 2, 1)], axis=0)
-        block[:, BLK:] = jnp.where(lane == columns - BLK, 1.0, both).astype(BF16)
+    lane = lax.broadcasted_iota(jnp.int32, (share, BLK), 1)
+
+    def unpack(step, at):
+        for k in range(SHARES):
+            span = slice(at + k * share, at + (k + 1) * share)
+            block[span, :BLK] = got[step, k, :share, :]
+            tails = got[step, k, share:, :].astype(F32)
+            both = jnp.concatenate([tails, pltpu.roll(tails, BLK // 2, 1)], axis=0)
+            block[span, BLK:] = jnp.where(lane == columns - BLK, 1.0, both).astype(BF16)
 
     pos = lax.broadcasted_iota(jnp.int32, (1, asks), 1)
 
@@ -163,14 +160,14 @@
         keys = slots_ref[:, pl.ds(pl.multiple_of(owner * asks, BLK), asks)]
         return jnp.where(pos < bc_ref[0, owner] * BLK, keys, -1)
 
-    target = lax.broadcasted_iota(jnp.int32, (rows_out, asks), 0) * REL
-
     def sums(keys, chunk, rel):
+        depth = keys.shape[1]
+        target = lax.broadcasted_iota(jnp.int32, (rows_out, depth), 0) * REL
         hits = target == keys - (chunk * rows_out * REL + rel)
         pick = jnp.where(hits, 1.0, 0.0).astype(BF16)
-        return jnp.dot(pick, block[...], preferred_element_type=F32)
-
-    unpack(steps)
+        return jnp.dot(pick, block[:depth, :], preferred_element_type=F32)
+
+    unpack(steps, 0)
     own_keys = keys_of(me)
 
     @pl.loop(0, 4)
@@ -178,10 +175,11 @@
         for rel in range(REL):
             agg[chunk, rel] = sums(own_keys, chunk, rel)
 
-    @pl.loop(0, steps - 1)
-    def _(step):
-        answer(step).wait_recv()
-        unpack(step)
+    @pl.loop(0, steps - 2)
+    def _(step):
+        for k in range(SHARES):
+            answer(step, k).wait_recv()
+        unpack(step, 0)
         keys = keys_of(owner_of(step))
 
         @pl.loop(0, 4)
@@ -189,9 +187,11 @@
             for rel in range(REL):
                 agg[chunk, rel] += sums(keys, chunk, rel)
 
-    answer(steps - 1).wait_recv()
-    unpack(steps - 1)
-    last_keys = keys_of(owner_of(steps - 1))
+    for i in range(2):
+        for k in range(SHARES):
+            answer(steps - 2 + i, k).wait_recv()
+        unpack(steps - 2 + i, i * asks)
+    last_keys = jnp.concatenate([keys_of(owner_of(steps - 2)), keys_of(owner_of(steps - 1))], axis=1)
 
     def operands(chunk):
         for rel in range(REL):
@@ -290,7 +290,8 @@
     @pl.loop(0, steps)
     def _(step):
         ask(step).wait_send()
-        answer(step).wait_send()
+        for k in range(SHARES):
+            answer(step, k).wait_send()
 
     for q in range(COL_PIECES):
         to_pair(0, q).wait_send()
@@ -308,7 +309,8 @@
     steps = owners - 1
     rows_out = 640 // ranks
     piece = width // COL_PIECES
-    packed = asks + asks // 2
+    share = asks // SHARES
+    packed = share + share // 2
     dma = pltpu.SemaphoreType.DMA
     vmem = pl.BlockSpec(memory_space=pltpu.VMEM)
     hbm = pl.BlockSpec(memory_space=pl.ANY)
@@ -322,10 +324,10 @@
             pltpu.VMEM((columns, nodes), BF16),
             pltpu.VMEM((nodes, columns), F32),
             pltpu.VMEM((rels, columns, width), BF16),
-            pltpu.VMEM((asks, columns), F32),
-            pltpu.VMEM((steps, packed, BLK), BF16),
-            pltpu.VMEM((owners, packed, BLK), BF16),
-            pltpu.VMEM((asks, 2 * BLK), BF16),
+            pltpu.VMEM((share, columns), F32),
+            pltpu.VMEM((steps, SHARES, packed, BLK), BF16),
+            pltpu.VMEM((owners, SHARES, packed, BLK), BF16),
+            pltpu.VMEM((2 * asks, 2 * BLK), BF16),
             pltpu.VMEM((ranks, REL, rows_out, 2 * BLK), F32),
             pltpu.VMEM((ranks, rows_out, width), F32),
             pltpu.VMEM((REL, rows_out, columns), BF16),
@@ -337,7 +339,7 @@
             pltpu.VMEM((COL_PIECES, 1, rows_out), F32),
             pltpu.VMEM((COL_PIECES, rows_out, piece), F32),
             dma((steps,)), dma((steps,)), dma((FEAT_CHUNKS,)), dma, dma,
-            dma((steps,)), dma((steps,)),
+            dma((steps, SHARES)), dma((steps, SHARES)),
             dma((2, COL_PIECES)), dma((2, COL_PIECES)),
             dma((COL_PIECES,)), dma((COL_PIECES,)), dma((COL_PIECES,)), dma((COL_PIECES,)),
         ],

time: 40.7 us -> 38.4 us (0.943)
  Pallas kernels: 38.8 us -> 36.5 us
    pallas_call x1, Pallas kernels: 38.8 us -> 36.5 us  [body(): pl.pallas_call(functools.partial(kernel, owners), out_shape=jax.ShapeDtyp...]
where the time goes in v4:
time: 38.4 us; the launch traced here: 38.2 us
  Pallas kernels  36.5 us (95%)
  local copies, waits for them, and re-layouts  1.72 us (4%)
    pallas_call x1, Pallas kernels, body(): pl.pallas_call(functools.partial(kernel, owners), out_shape=jax.ShapeDtyp...  36.5 us
    unnamed x1, local copies, waits for them, and re-layouts  1.72 us

profile of v4, /device:TPU:0, one launch (start us, length us, event | category | flops | bytes accessed | tf_op | source)
XLA Modules:
  0.0 38.2 jit_solution(14256374755406963839)
XLA Ops:
  0.0 36.5 %rgcn.1 = bf16[160,1024]{1,0:T(8,128)(2,1)} custom-call(s32[1,4]{1,0:T(1,128)} %bc_ref.1, s32[1,1536]{1,0:T(1,128)} %rows_ref.1, s32[1,1536]{1,0:T(1,128)} %slots_ref.1, bf16[192,8192]{1,0:T(8,128)(2,1)} %bitcast.4, bf16[6,192,1024]{2,1,0:T(8,128)(2,1)} %weight_ref.1, f32[1,1024]{1,0:T(1,128)} %bitcast.5, f32[1,1024]{1,0:T(1,128)} %bitcast.6, f32[1,1024]{1,0:T(1,128)} %bitcast.7), custom_call_target="tpu_custom_call" | custom-call | tf_op jit(solution)/shard_map/rgcn/pallas_call | solution.py:317
  36.5 1.7 %copy.10 = bf16[160,1024]{1,0:T(8,128)(2,1)} copy(bf16[160,1024]{1,0:T(8,128)(2,1)} %rgcn.1) | data formatting | bytes 655360

commit v5 on v4

--- a/solution.py
+++ b/solution.py
@@ -19,14 +19,15 @@
 CAST_ROWS = 256
 GATHER_UNROLL = 16
 COL_PIECES = 4
-SHARES = 2
+SHARES = 3
 LEVELS = 32767.0
 TINY = 1e-30
 
 
 def kernel(
-    owners, bc_ref, rows_ref, slots_ref, feats_ref, weight_ref, bias_ref, gain_ref, offset_ref,
+    owners, bc_hbm, rows_ref, slots_hbm, feats_ref, weight_ref, bias_hbm, gain_hbm, offset_hbm,
     out_ref,
+    bc_ref, slots_ref, bias_ref, gain_ref, offset_ref, small_sem,
     asked, feats_v, feats_f, weight_v, found, sent, got, block, agg, own_term, operand,
     part, half_in, half_out, half_scale, last_in, last_scale, acted,
     asked_send, asked_recv, feats_sem, weight_sem, own_sem, row_send, row_recv,
@@ -38,7 +39,7 @@
     pair = {"feat": high * 2 + 1 - low}
     far = {"feat": (1 - high) * 2 + low}
     nodes, columns = feats_f.shape
-    asks = slots_ref.shape[1] // owners
+    asks = rows_ref.shape[1] // owners
     share = asks // SHARES
     half = share // 2
     steps = owners - 1
@@ -57,6 +58,14 @@
     def my_rows(owner):
         return rows_ref.at[:, pl.ds(pl.multiple_of(owner * asks, BLK), asks)]
 
+    barrier = pltpu.get_barrier_semaphore()
+
+    @pl.loop(0, steps)
+    def _(step):
+        pl.semaphore_signal(barrier, inc=1, device_id={"row": dest_of(step)}, device_id_type=MESH)
+
+    pl.semaphore_signal(barrier, inc=1, device_id=pair, device_id_type=MESH)
+    pl.semaphore_signal(barrier, inc=1, device_id=far, device_id_type=MESH)
     chunk_rows = nodes // FEAT_CHUNKS
 
     def feats_copy(c):
@@ -69,16 +78,15 @@
     own_copy.start()
     weight_copy = pltpu.make_async_copy(weight_ref, weight_v, weight_sem)
     weight_copy.start()
-
-    barrier = pltpu.get_barrier_semaphore()
-
-    @pl.loop(0, steps)
-    def _(step):
-        pl.semaphore_signal(barrier, inc=1, device_id={"row": dest_of(step)}, device_id_type=MESH)
-
-    pl.semaphore_signal(barrier, inc=1, device_id=pair, device_id_type=MESH)
-    pl.semaphore_signal(barrier, inc=1, device_id=far, device_id_type=MESH)
-    pl.semaphore_wait(barrier, steps + 2)
+    small = [
+        pltpu.make_async_copy(src, dst, small_sem.at[i])
+        for i, (src, dst) in enumerate([
+            (bc_hbm, bc_ref), (slots_hbm, slots_ref), (bias_hbm, bias_ref),
+            (gain_hbm, gain_ref), (offset_hbm, offset_ref),
+        ])
+    ]
+    for copy in small:
+        copy.start()
 
     def ask(step):
         owner = owner_of(step)
@@ -95,16 +103,11 @@
             device_id={"row": dest_of(step)}, device_id_type=MESH,
         )
 
-    @pl.loop(0, steps)
-    def _(step):
-        ask(step).start()
-
     unit_row = lax.broadcasted_iota(jnp.int32, (CAST_ROWS, CAST_ROWS), 0)
     unit_col = lax.broadcasted_iota(jnp.int32, (CAST_ROWS, CAST_ROWS), 1)
     unit = jnp.where(unit_row == unit_col, 1.0, 0.0).astype(BF16)
 
-    @pl.loop(0, FEAT_CHUNKS)
-    def _(c):
+    def turn(c):
         feats_copy(c).wait()
 
         for i in range(chunk_rows // CAST_ROWS):
@@ -112,6 +115,15 @@
             feats_f[span, :] = lax.dot_general(
                 unit, feats_v[:, span], (((1,), (1,)), ((), ())), preferred_element_type=F32
             )
+
+    pl.loop(0, FEAT_CHUNKS // 2)(turn)
+    pl.semaphore_wait(barrier, steps + 2)
+
+    @pl.loop(0, steps)
+    def _(step):
+        ask(step).start()
+
+    pl.loop(FEAT_CHUNKS // 2, FEAT_CHUNKS)(turn)
 
     def gather(step, k, to):
         @pl.loop(0, share // GATHER_UNROLL)
@@ -126,18 +138,20 @@
         second = found[half:, BLK:]
         to[step, k, share:, :] = jnp.concatenate([first, second], axis=1).astype(BF16)
 
-    @pl.loop(0, steps)
-    def _(step):
-        ask(step).wait_recv()
-        for k in range(SHARES):
-            gather(step, k, sent)
-            answer(step, k).start()
-
     own_copy.wait()
     for k in range(SHARES):
         gather(steps, k, got)
 
+    @pl.loop(0, steps)
+    def _(step):
+        ask(step).wait_recv()
+        for k in range(SHARES):
+            gather(step, k, sent)
+            answer(step, k).start()
+
     weight_copy.wait()
+    for copy in small:
+        copy.wait()
 
     @pl.loop(0, 4)
     def _(c):
@@ -317,9 +331,15 @@
     return pl.pallas_call(
         functools.partial(kernel, owners),
         out_shape=jax.ShapeDtypeStruct((rows_out, width), BF16),
-        in_specs=[pl.BlockSpec(memory_space=pltpu.SMEM), hbm, vmem, hbm, hbm, vmem, vmem, vmem],
+        in_specs=[hbm] * 8,
         out_specs=vmem,
         scratch_shapes=[
+            pltpu.SMEM(block_count.shape, jnp.int32),
+            pltpu.VMEM(req_slots.shape, jnp.int32),
+            pltpu.VMEM((1, width), F32),
+            pltpu.VMEM((1, width), F32),
+            pltpu.VMEM((1, width), F32),
+            dma((5,)),
             pltpu.SMEM((owners, 1, asks), jnp.int32),
             pltpu.VMEM((columns, nodes), BF16),
             pltpu.VMEM((nodes, columns), F32),
@@ -344,7 +364,7 @@
             dma((COL_PIECES,)), dma((COL_PIECES,)), dma((COL_PIECES,)), dma((COL_PIECES,)),
         ],
         compiler_params=pltpu.CompilerParams(
-            collective_id=0, has_side_effects=True, vmem_limit_bytes=60 * 1024 * 1024
+            collective_id=0, has_side_effects=True, vmem_limit_bytes=58 * 1024 * 1024
         ),
         name="rgcn",
     )(

time: 38.4 us -> 37.5 us (0.977)
  Pallas kernels: 36.5 us -> 35.6 us
    pallas_call x1, Pallas kernels: 36.5 us -> 35.6 us  [body(): pl.pallas_call(functools.partial(kernel, owners), out_shape=jax.ShapeDtyp...]
where the time goes in v5:
time: 37.5 us; the launch traced here: 37.3 us
  Pallas kernels  35.6 us (95%)
  local copies, waits for them, and re-layouts  1.72 us (5%)
    pallas_call x1, Pallas kernels, body(): pl.pallas_call(functools.partial(kernel, owners), out_shape=jax.ShapeDtyp...  35.6 us
    unnamed x1, local copies, waits for them, and re-layouts  1.72 us

profile of v5, /device:TPU:0, one launch (start us, length us, event | category | flops | bytes accessed | tf_op | source)
XLA Modules:
  0.0 37.3 jit_solution(17794356150381897472)
XLA Ops:
  0.0 35.6 %rgcn.1 = bf16[160,1024]{1,0:T(8,128)(2,1)} custom-call(s32[1,4]{1,0:T(1,128)} %bc_hbm.1, s32[1,1536]{1,0:T(1,128)} %rows_ref.1, s32[1,1536]{1,0:T(1,128)} %slots_hbm.1, bf16[192,8192]{1,0:T(8,128)(2,1)} %bitcast.4, bf16[6,192,1024]{2,1,0:T(8,128)(2,1)} %weight_ref.1, f32[1,1024]{1,0:T(1,128)} %bitcast.5, f32[1,1024]{1,0:T(1,128)} %bitcast.6, f32[1,1024]{1,0:T(1,128)} %bitcast.7), custom_call_target="tpu_custom_call" | custom-call | tf_op jit(solution)/shard_map/rgcn/pallas_call | solution.py:331
  35.6 1.7 %copy.10 = bf16[160,1024]{1,0:T(8,128)(2,1)} copy(bf16[160,1024]{1,0:T(8,128)(2,1)} %rgcn.1) | data formatting | bytes 655360
